TPU v7x, 32 devices: a whole 2x2x4 slice. The times are simulated.
32 devices in a mesh: ctx: 8 (over z, y), tp: 4 (over x, core).
Axes of the slice: x: 2, y: 2, z: 4, core: 2. Of those that a mesh axis runs over, the one named last changes fastest.
Arguments:
- query_proj: bfloat16 [2048, 8192], P('ctx', 'tp'), may hold values from -24 to 24, as said below
- key_proj: bfloat16 [2048, 8192], P('ctx', 'tp'), may hold values from -6 to 6
- value_proj: bfloat16 [2048, 8192], P('ctx', 'tp'), may hold values from -6 to 6
- filters: bfloat16 [128, 8192], P(None, 'tp'), may hold values from -6 to 6, as said below
- norm_gain: float32 [8192], P('tp'), may hold values from 0.1 to 1.9
- grad_out: bfloat16 [2048, 8192], P('ctx', 'tp'), may hold values from -6 to 6
Outputs:
- mixed: bfloat16 [2048, 8192], P('ctx', 'tp')
- grad_query: bfloat16 [2048, 8192], P('ctx', 'tp')
- grad_key: bfloat16 [2048, 8192], P('ctx', 'tp')
- grad_value: bfloat16 [2048, 8192], P('ctx', 'tp')
- grad_filter: float32 [128, 8192], P(None, 'tp')
- grad_gain: float32 [8192], P('tp')
Inputs may be any that keep to these rules, and one draw needn't show every extreme that they name: `query_proj`: finite real values. `filters`: finite real values.
All inputs are finite; a program needn't handle non-finite values.
Results may differ from a plain program's by a relative error of at most 0.0051.
Values may be sent and summed in bfloat16 or wider, within the bound.
A program may use at most 64 MiB of HBM per device.

v0:
```python
import math

import jax
import jax.numpy as jnp
from jax import lax
from jax.sharding import PartitionSpec as P

EPS = 1e-06


def passed_along(array, axis, by):
    length = lax.axis_size(axis)
    pairs = [(i, i + by) for i in range(length) if 0 <= i + by < length]
    return lax.ppermute(array, axis, pairs)


def tap_sum(extended, weights, row_count, causal):
    tap_count = weights.shape[0]

    def tap_group_step(group_index, running):
        for offset in range(16):
            tap_index = group_index * 16 + offset
            first_row = tap_count - 1 - tap_index if causal else tap_index
            window = lax.dynamic_slice_in_dim(extended, first_row, row_count, 0).astype(jnp.float32)
            running = running + weights[tap_index] * window
        return running

    return lax.fori_loop(
        0, tap_count // 16, tap_group_step, jnp.zeros((row_count, extended.shape[1]), jnp.float32)
    )


def filter_grad(grad_conv, extended, tap_count):
    row_count = grad_conv.shape[0]

    def filter_group_step(group_index, total):
        rows_out = []
        for offset in range(16):
            tap_index = group_index * 16 + offset
            window = lax.dynamic_slice_in_dim(extended, tap_count - 1 - tap_index, row_count, 0)
            rows_out.append(jnp.sum(grad_conv.astype(jnp.float32) * window.astype(jnp.float32), 0))
        return lax.dynamic_update_slice_in_dim(total, jnp.stack(rows_out), group_index * 16, 0)

    return lax.fori_loop(
        0,
        tap_count // 16,
        filter_group_step,
        jnp.zeros((tap_count, grad_conv.shape[1]), jnp.float32),
    )


def on_device(query_proj, key_proj, value_proj, filters, norm_gain, grad_out):
    row_count, col_count = query_proj.shape
    tap_count = filters.shape[0]
    rim_rows = tap_count - 1
    width = col_count * lax.axis_size("tp")
    scale = 1.0 / math.sqrt(row_count * lax.axis_size("ctx"))
    filt_wide = filters.astype(jnp.float32)
    key_wide = key_proj.astype(jnp.float32)
    value_wide = value_proj.astype(jnp.float32)
    query_wide = query_proj.astype(jnp.float32)
    key_value = (key_wide * value_wide).astype(jnp.bfloat16)
    before = passed_along(key_value[row_count - rim_rows :], "ctx", 1)
    kv_ext = jnp.concatenate([before, key_value], 0)
    conv_out = tap_sum(kv_ext, filt_wide, row_count, True)
    gated = query_wide * conv_out
    row_sq = lax.psum(jnp.sum(gated * gated, 1), "tp")
    row_rms = jnp.sqrt(row_sq / width + EPS)
    normed = gated / row_rms[:, None]
    mixed = (normed * norm_gain).astype(jnp.bfloat16)
    grad_wide = grad_out.astype(jnp.float32)
    grad_scaled = grad_wide * norm_gain
    row_mean = lax.psum(jnp.sum(grad_scaled * normed, 1), "tp") / width
    grad_gated = (grad_scaled - normed * row_mean[:, None]) / row_rms[:, None]
    grad_query = (grad_gated * conv_out).astype(jnp.bfloat16)
    grad_conv = (grad_gated * query_wide).astype(jnp.bfloat16)
    after = passed_along(grad_conv[:rim_rows], "ctx", -1)
    grad_ext = jnp.concatenate([grad_conv, after], 0)
    grad_kv = tap_sum(grad_ext, filt_wide, row_count, False)
    grad_key = (grad_kv * value_wide).astype(jnp.bfloat16)
    grad_value = (grad_kv * key_wide).astype(jnp.bfloat16)
    filter_local = filter_grad(grad_conv, kv_ext, tap_count)
    gain_local = jnp.sum(grad_wide * normed, 0)
    filter_total, gain_total = lax.psum((filter_local, gain_local), "ctx")
    return (mixed, grad_query, grad_key, grad_value, filter_total * scale, gain_total * scale)


def solution(mesh):
    placed = (
        P("ctx", "tp"),
        P("ctx", "tp"),
        P("ctx", "tp"),
        P(None, "tp"),
        P("tp"),
        P("ctx", "tp"),
    )
    return jax.shard_map(
        on_device,
        mesh=mesh,
        in_specs=placed,
        out_specs=(
            P("ctx", "tp"),
            P("ctx", "tp"),
            P("ctx", "tp"),
            P("ctx", "tp"),
            P(None, "tp"),
            P("tp"),
        ),
        check_vma=False,
    )
```

profile of v0, /device:TPU:0, one launch (start us, length us, event | category | flops | bytes accessed | tf_op | source)
XLA Modules:
  0.0 335.7 jit_solution(14680146612777388618)
XLA Ops:
  9.3 4.9 %collective-permute-start = (bf16[127,2048]{1,0:T(8,128)(2,1)S(1)}, bf16[127,2048]{1,0:T(8,128)(2,1)S(1)}, u32[]{:S(2)}, u32[]{:S(2)}) collective-permute-start(bf16[127,2048]{1,0:T(8,128)(2,1)S(1)} %slice.8), channel_id=1, source_target_pairs={{0,4},{4,8},{8,12},{12,16},{16,20},{20,24},{24,28},{1,5},{5,9},{9,... | collective-permute-start | bytes 1560584 | tf_op jit(solution)/shard_map/ppermute | solution.py:14
  15.4 10.0 %collective-permute-done = bf16[127,2048]{1,0:T(8,128)(2,1)S(1)} collective-permute-done((bf16[127,2048]{1,0:T(8,128)(2,1)S(1)}, bf16[127,2048]{1,0:T(8,128)(2,1)S(1)}, u32[]{:S(2)}, u32[]{:S(2)}) %collective-permute-start) | collective-permute-done | bytes 520224 | tf_op jit(solution)/shard_map/ppermute | solution.py:14
  25.7 87.3 %while.50 = (s32[]{:T(128)}, f32[256,2048]{1,0:T(8,128)}, f32[128,2048]{1,0:T(8,128)}, bf16[383,2048]{1,0:T(8,128)(2,1)S(1)}, s32[]{:T(128)}, /*index=5*/s32[]{:...) while((s32[]{:T(128)}, f32[256,2048]{1,0:T(8,128)}, ...), condition=%wide.region_1.0_spmd.clone, body=%wide.region_0.0_spmd.clone.sunk | while | flops 25690244 | bytes 21366684 | solution.py:28
  27.8 7.7 %fusion.60 = f32[256,2048]{1,0:T(8,128)} fusion(f32[256,2048]{1,0:T(8,128)} %get-tuple-element.789, bf16[383,2048]{1,0:T(8,128)(2,1)S(1)} %get-tuple-element.830, s32[]{:T(128)S(6)} %select_n.1021, f32[2048]{0:T(1024)S(1)} %bitcast.145, s32[]{:T(128)S(6)} %select_n.1038, f32[2048]{0:T(1024)S(1)} %bitcast.146, s32[]{:T(128)S(6)} %select_n.1039, ...), kind=kLoop, calls=%fused_computation.48.clone.1 | loop fusion | flops 25690112 | bytes 21102656 | tf_op jit(solution)/shard_map/while/body/eval_jaxpr/add | solution.py:25
  37.4 9.3 %fusion.60 = f32[256,2048]{1,0:T(8,128)} fusion(f32[256,2048]{1,0:T(8,128)} %get-tuple-element.789, bf16[383,2048]{1,0:T(8,128)(2,1)S(1)} %get-tuple-element.830, s32[]{:T(128)S(6)} %select_n.1021, f32[2048]{0:T(1024)S(1)} %bitcast.145, s32[]{:T(128)S(6)} %select_n.1038, f32[2048]{0:T(1024)S(1)} %bitcast.146, s32[]{:T(128)S(6)} %select_n.1039, ...), kind=kLoop, calls=%fused_computation.48.clone.1 | loop fusion | flops 25690112 | bytes 21102656 | tf_op jit(solution)/shard_map/while/body/eval_jaxpr/add | solution.py:25
  48.3 9.3 %fusion.60 = f32[256,2048]{1,0:T(8,128)} fusion(f32[256,2048]{1,0:T(8,128)} %get-tuple-element.789, bf16[383,2048]{1,0:T(8,128)(2,1)S(1)} %get-tuple-element.830, s32[]{:T(128)S(6)} %select_n.1021, f32[2048]{0:T(1024)S(1)} %bitcast.145, s32[]{:T(128)S(6)} %select_n.1038, f32[2048]{0:T(1024)S(1)} %bitcast.146, s32[]{:T(128)S(6)} %select_n.1039, ...), kind=kLoop, calls=%fused_computation.48.clone.1 | loop fusion | flops 25690112 | bytes 21102656 | tf_op jit(solution)/shard_map/while/body/eval_jaxpr/add | solution.py:25
  59.4 9.3 %fusion.60 = f32[256,2048]{1,0:T(8,128)} fusion(f32[256,2048]{1,0:T(8,128)} %get-tuple-element.789, bf16[383,2048]{1,0:T(8,128)(2,1)S(1)} %get-tuple-element.830, s32[]{:T(128)S(6)} %select_n.1021, f32[2048]{0:T(1024)S(1)} %bitcast.145, s32[]{:T(128)S(6)} %select_n.1038, f32[2048]{0:T(1024)S(1)} %bitcast.146, s32[]{:T(128)S(6)} %select_n.1039, ...), kind=kLoop, calls=%fused_computation.48.clone.1 | loop fusion | flops 25690112 | bytes 21102656 | tf_op jit(solution)/shard_map/while/body/eval_jaxpr/add | solution.py:25
  70.7 9.3 %fusion.60 = f32[256,2048]{1,0:T(8,128)} fusion(f32[256,2048]{1,0:T(8,128)} %get-tuple-element.789, bf16[383,2048]{1,0:T(8,128)(2,1)S(1)} %get-tuple-element.830, s32[]{:T(128)S(6)} %select_n.1021, f32[2048]{0:T(1024)S(1)} %bitcast.145, s32[]{:T(128)S(6)} %select_n.1038, f32[2048]{0:T(1024)S(1)} %bitcast.146, s32[]{:T(128)S(6)} %select_n.1039, ...), kind=kLoop, calls=%fused_computation.48.clone.1 | loop fusion | flops 25690112 | bytes 21102656 | tf_op jit(solution)/shard_map/while/body/eval_jaxpr/add | solution.py:25
  81.9 9.3 %fusion.60 = f32[256,2048]{1,0:T(8,128)} fusion(f32[256,2048]{1,0:T(8,128)} %get-tuple-element.789, bf16[383,2048]{1,0:T(8,128)(2,1)S(1)} %get-tuple-element.830, s32[]{:T(128)S(6)} %select_n.1021, f32[2048]{0:T(1024)S(1)} %bitcast.145, s32[]{:T(128)S(6)} %select_n.1038, f32[2048]{0:T(1024)S(1)} %bitcast.146, s32[]{:T(128)S(6)} %select_n.1039, ...), kind=kLoop, calls=%fused_computation.48.clone.1 | loop fusion | flops 25690112 | bytes 21102656 | tf_op jit(solution)/shard_map/while/body/eval_jaxpr/add | solution.py:25
  92.8 9.3 %fusion.60 = f32[256,2048]{1,0:T(8,128)} fusion(f32[256,2048]{1,0:T(8,128)} %get-tuple-element.789, bf16[383,2048]{1,0:T(8,128)(2,1)S(1)} %get-tuple-element.830, s32[]{:T(128)S(6)} %select_n.1021, f32[2048]{0:T(1024)S(1)} %bitcast.145, s32[]{:T(128)S(6)} %select_n.1038, f32[2048]{0:T(1024)S(1)} %bitcast.146, s32[]{:T(128)S(6)} %select_n.1039, ...), kind=kLoop, calls=%fused_computation.48.clone.1 | loop fusion | flops 25690112 | bytes 21102656 | tf_op jit(solution)/shard_map/while/body/eval_jaxpr/add | solution.py:25
  103.7 9.3 %fusion.60 = f32[256,2048]{1,0:T(8,128)} fusion(f32[256,2048]{1,0:T(8,128)} %get-tuple-element.789, bf16[383,2048]{1,0:T(8,128)(2,1)S(1)} %get-tuple-element.830, s32[]{:T(128)S(6)} %select_n.1021, f32[2048]{0:T(1024)S(1)} %bitcast.145, s32[]{:T(128)S(6)} %select_n.1038, f32[2048]{0:T(1024)S(1)} %bitcast.146, s32[]{:T(128)S(6)} %select_n.1039, ...), kind=kLoop, calls=%fused_computation.48.clone.1 | loop fusion | flops 25690112 | bytes 21102656 | tf_op jit(solution)/shard_map/while/body/eval_jaxpr/add | solution.py:25
  115.0 5.7 %psum.28 = f32[256]{0:T(256)S(1)} all-reduce(f32[256]{0:T(256)S(1)} %multiply_reduce_fusion), channel_id=1, replica_groups=mesh['ctx'=8,'tp'=4] {'tp'}, use_global_device_ids=true, to_apply=%region_3.0 | all-reduce | flops 256 | bytes 2048 | tf_op jit(solution)/shard_map/psum | solution.py:67
  123.5 6.6 %psum.29 = f32[256]{0:T(256)S(1)} all-reduce(f32[256]{0:T(256)S(1)} %get-tuple-element.516), channel_id=1, replica_groups=mesh['ctx'=8,'tp'=4] {'tp'}, use_global_device_ids=true, to_apply=%region_5.0 | all-reduce | flops 256 | bytes 2048 | tf_op jit(solution)/shard_map/psum | solution.py:73
  137.4 69.4 %while.49 = (s32[]{:T(128)}, f32[128,2048]{1,0:T(8,128)}, bf16[256,2048]{1,0:T(8,128)(2,1)S(1)}, bf16[383,2048]{1,0:T(8,128)(2,1)S(1)}, s32[]{:T(128)}, /*index=...) while((s32[]{:T(128)}, f32[128,2048]{1,0:T(8,128)}, ...), condition=%wide.region_25.0_spmd, body=%wide.region_8.0_spmd.sunk | while | flops 25657424 | bytes 18482392 | solution.py:44
  137.4 7.8 %fusion.59 = (f32[2048]{0:T(1024)S(1)}, f32[2048]{0:T(1024)S(1)}, f32[2048]{0:T(1024)S(1)}, f32[2048]{0:T(1024)S(1)}, f32[2048]{0:T(1024)S(1)}, /*index=5*/f32[2...) fusion(bf16[256,2048]{1,0:T(8,128)(2,1)S(1)} %get-tuple-element, ...), kind=kLoop, calls=%fused_computation.31.clone.1 | loop fusion | flops 25657344 | bytes 17956928 | tf_op jit(solution)/shard_map/while/body/eval_jaxpr/reduce_sum | solution.py:41
  146.1 7.8 %fusion.59 = (f32[2048]{0:T(1024)S(1)}, f32[2048]{0:T(1024)S(1)}, f32[2048]{0:T(1024)S(1)}, f32[2048]{0:T(1024)S(1)}, f32[2048]{0:T(1024)S(1)}, /*index=5*/f32[2...) fusion(bf16[256,2048]{1,0:T(8,128)(2,1)S(1)} %get-tuple-element, ...), kind=kLoop, calls=%fused_computation.31.clone.1 | loop fusion | flops 25657344 | bytes 17956928 | tf_op jit(solution)/shard_map/while/body/eval_jaxpr/reduce_sum | solution.py:41
  154.8 7.8 %fusion.59 = (f32[2048]{0:T(1024)S(1)}, f32[2048]{0:T(1024)S(1)}, f32[2048]{0:T(1024)S(1)}, f32[2048]{0:T(1024)S(1)}, f32[2048]{0:T(1024)S(1)}, /*index=5*/f32[2...) fusion(bf16[256,2048]{1,0:T(8,128)(2,1)S(1)} %get-tuple-element, ...), kind=kLoop, calls=%fused_computation.31.clone.1 | loop fusion | flops 25657344 | bytes 17956928 | tf_op jit(solution)/shard_map/while/body/eval_jaxpr/reduce_sum | solution.py:41
  163.5 7.8 %fusion.59 = (f32[2048]{0:T(1024)S(1)}, f32[2048]{0:T(1024)S(1)}, f32[2048]{0:T(1024)S(1)}, f32[2048]{0:T(1024)S(1)}, f32[2048]{0:T(1024)S(1)}, /*index=5*/f32[2...) fusion(bf16[256,2048]{1,0:T(8,128)(2,1)S(1)} %get-tuple-element, ...), kind=kLoop, calls=%fused_computation.31.clone.1 | loop fusion | flops 25657344 | bytes 17956928 | tf_op jit(solution)/shard_map/while/body/eval_jaxpr/reduce_sum | solution.py:41
  172.1 7.8 %fusion.59 = (f32[2048]{0:T(1024)S(1)}, f32[2048]{0:T(1024)S(1)}, f32[2048]{0:T(1024)S(1)}, f32[2048]{0:T(1024)S(1)}, f32[2048]{0:T(1024)S(1)}, /*index=5*/f32[2...) fusion(bf16[256,2048]{1,0:T(8,128)(2,1)S(1)} %get-tuple-element, ...), kind=kLoop, calls=%fused_computation.31.clone.1 | loop fusion | flops 25657344 | bytes 17956928 | tf_op jit(solution)/shard_map/while/body/eval_jaxpr/reduce_sum | solution.py:41
  180.8 7.8 %fusion.59 = (f32[2048]{0:T(1024)S(1)}, f32[2048]{0:T(1024)S(1)}, f32[2048]{0:T(1024)S(1)}, f32[2048]{0:T(1024)S(1)}, f32[2048]{0:T(1024)S(1)}, /*index=5*/f32[2...) fusion(bf16[256,2048]{1,0:T(8,128)(2,1)S(1)} %get-tuple-element, ...), kind=kLoop, calls=%fused_computation.31.clone.1 | loop fusion | flops 25657344 | bytes 17956928 | tf_op jit(solution)/shard_map/while/body/eval_jaxpr/reduce_sum | solution.py:41
  189.5 7.8 %fusion.59 = (f32[2048]{0:T(1024)S(1)}, f32[2048]{0:T(1024)S(1)}, f32[2048]{0:T(1024)S(1)}, f32[2048]{0:T(1024)S(1)}, f32[2048]{0:T(1024)S(1)}, /*index=5*/f32[2...) fusion(bf16[256,2048]{1,0:T(8,128)(2,1)S(1)} %get-tuple-element, ...), kind=kLoop, calls=%fused_computation.31.clone.1 | loop fusion | flops 25657344 | bytes 17956928 | tf_op jit(solution)/shard_map/while/body/eval_jaxpr/reduce_sum | solution.py:41
  198.1 7.8 %fusion.59 = (f32[2048]{0:T(1024)S(1)}, f32[2048]{0:T(1024)S(1)}, f32[2048]{0:T(1024)S(1)}, f32[2048]{0:T(1024)S(1)}, f32[2048]{0:T(1024)S(1)}, /*index=5*/f32[2...) fusion(bf16[256,2048]{1,0:T(8,128)(2,1)S(1)} %get-tuple-element, ...), kind=kLoop, calls=%fused_computation.31.clone.1 | loop fusion | flops 25657344 | bytes 17956928 | tf_op jit(solution)/shard_map/while/body/eval_jaxpr/reduce_sum | solution.py:41
  206.9 26.1 %psum.31 = f32[2048]{0:T(1024)S(1)} all-reduce(f32[2048]{0:T(1024)S(1)} %get-tuple-element.515), channel_id=1, replica_groups=mesh['ctx'=8,'tp'=4] {'ctx'}, use_global_device_ids=true, to_apply=%region_28.0 | all-reduce | flops 2048 | bytes 16384 | tf_op jit(solution)/shard_map/psum | solution.py:84
  234.7 88.1 %while.51 = (s32[]{:T(128)}, f32[256,2048]{1,0:T(8,128)}, f32[128,2048]{1,0:T(8,128)}, bf16[383,2048]{1,0:T(8,128)(2,1)S(1)}, s32[]{:T(128)}, /*index=5*/s32[]{:...) while((s32[]{:T(128)}, f32[256,2048]{1,0:T(8,128)}, ...), condition=%wide.region_7.0_spmd.clone, body=%wide.region_6.0_spmd.clone.sunk | while | flops 25690212 | bytes 21366460 | solution.py:28
  236.8 7.8 %fusion.61 = f32[256,2048]{1,0:T(8,128)} fusion(f32[256,2048]{1,0:T(8,128)} %get-tuple-element.920, bf16[383,2048]{1,0:T(8,128)(2,1)S(1)} %get-tuple-element.975, s32[]{:T(128)S(6)} %select_n.1053, f32[2048]{0:T(1024)S(1)} %bitcast.161, s32[]{:T(128)S(6)} %select_n.1070, f32[2048]{0:T(1024)S(1)} %bitcast.162, s32[]{:T(128)S(6)} %select_n.1071, ...), kind=kLoop, calls=%fused_computation.80.clone.1 | loop fusion | flops 25690112 | bytes 21102656 | tf_op jit(solution)/shard_map/while/body/eval_jaxpr/add | solution.py:25
  246.5 9.4 %fusion.61 = f32[256,2048]{1,0:T(8,128)} fusion(f32[256,2048]{1,0:T(8,128)} %get-tuple-element.920, bf16[383,2048]{1,0:T(8,128)(2,1)S(1)} %get-tuple-element.975, s32[]{:T(128)S(6)} %select_n.1053, f32[2048]{0:T(1024)S(1)} %bitcast.161, s32[]{:T(128)S(6)} %select_n.1070, f32[2048]{0:T(1024)S(1)} %bitcast.162, s32[]{:T(128)S(6)} %select_n.1071, ...), kind=kLoop, calls=%fused_computation.80.clone.1 | loop fusion | flops 25690112 | bytes 21102656 | tf_op jit(solution)/shard_map/while/body/eval_jaxpr/add | solution.py:25
  257.5 9.4 %fusion.61 = f32[256,2048]{1,0:T(8,128)} fusion(f32[256,2048]{1,0:T(8,128)} %get-tuple-element.920, bf16[383,2048]{1,0:T(8,128)(2,1)S(1)} %get-tuple-element.975, s32[]{:T(128)S(6)} %select_n.1053, f32[2048]{0:T(1024)S(1)} %bitcast.161, s32[]{:T(128)S(6)} %select_n.1070, f32[2048]{0:T(1024)S(1)} %bitcast.162, s32[]{:T(128)S(6)} %select_n.1071, ...), kind=kLoop, calls=%fused_computation.80.clone.1 | loop fusion | flops 25690112 | bytes 21102656 | tf_op jit(solution)/shard_map/while/body/eval_jaxpr/add | solution.py:25
  268.7 9.4 %fusion.61 = f32[256,2048]{1,0:T(8,128)} fusion(f32[256,2048]{1,0:T(8,128)} %get-tuple-element.920, bf16[383,2048]{1,0:T(8,128)(2,1)S(1)} %get-tuple-element.975, s32[]{:T(128)S(6)} %select_n.1053, f32[2048]{0:T(1024)S(1)} %bitcast.161, s32[]{:T(128)S(6)} %select_n.1070, f32[2048]{0:T(1024)S(1)} %bitcast.162, s32[]{:T(128)S(6)} %select_n.1071, ...), kind=kLoop, calls=%fused_computation.80.clone.1 | loop fusion | flops 25690112 | bytes 21102656 | tf_op jit(solution)/shard_map/while/body/eval_jaxpr/add | solution.py:25
  280.0 9.4 %fusion.61 = f32[256,2048]{1,0:T(8,128)} fusion(f32[256,2048]{1,0:T(8,128)} %get-tuple-element.920, bf16[383,2048]{1,0:T(8,128)(2,1)S(1)} %get-tuple-element.975, s32[]{:T(128)S(6)} %select_n.1053, f32[2048]{0:T(1024)S(1)} %bitcast.161, s32[]{:T(128)S(6)} %select_n.1070, f32[2048]{0:T(1024)S(1)} %bitcast.162, s32[]{:T(128)S(6)} %select_n.1071, ...), kind=kLoop, calls=%fused_computation.80.clone.1 | loop fusion | flops 25690112 | bytes 21102656 | tf_op jit(solution)/shard_map/while/body/eval_jaxpr/add | solution.py:25
  291.4 9.4 %fusion.61 = f32[256,2048]{1,0:T(8,128)} fusion(f32[256,2048]{1,0:T(8,128)} %get-tuple-element.920, bf16[383,2048]{1,0:T(8,128)(2,1)S(1)} %get-tuple-element.975, s32[]{:T(128)S(6)} %select_n.1053, f32[2048]{0:T(1024)S(1)} %bitcast.161, s32[]{:T(128)S(6)} %select_n.1070, f32[2048]{0:T(1024)S(1)} %bitcast.162, s32[]{:T(128)S(6)} %select_n.1071, ...), kind=kLoop, calls=%fused_computation.80.clone.1 | loop fusion | flops 25690112 | bytes 21102656 | tf_op jit(solution)/shard_map/while/body/eval_jaxpr/add | solution.py:25
  302.4 9.4 %fusion.61 = f32[256,2048]{1,0:T(8,128)} fusion(f32[256,2048]{1,0:T(8,128)} %get-tuple-element.920, bf16[383,2048]{1,0:T(8,128)(2,1)S(1)} %get-tuple-element.975, s32[]{:T(128)S(6)} %select_n.1053, f32[2048]{0:T(1024)S(1)} %bitcast.161, s32[]{:T(128)S(6)} %select_n.1070, f32[2048]{0:T(1024)S(1)} %bitcast.162, s32[]{:T(128)S(6)} %select_n.1071, ...), kind=kLoop, calls=%fused_computation.80.clone.1 | loop fusion | flops 25690112 | bytes 21102656 | tf_op jit(solution)/shard_map/while/body/eval_jaxpr/add | solution.py:25
  313.4 9.4 %fusion.61 = f32[256,2048]{1,0:T(8,128)} fusion(f32[256,2048]{1,0:T(8,128)} %get-tuple-element.920, bf16[383,2048]{1,0:T(8,128)(2,1)S(1)} %get-tuple-element.975, s32[]{:T(128)S(6)} %select_n.1053, f32[2048]{0:T(1024)S(1)} %bitcast.161, s32[]{:T(128)S(6)} %select_n.1070, f32[2048]{0:T(1024)S(1)} %bitcast.162, s32[]{:T(128)S(6)} %select_n.1071, ...), kind=kLoop, calls=%fused_computation.80.clone.1 | loop fusion | flops 25690112 | bytes 21102656 | tf_op jit(solution)/shard_map/while/body/eval_jaxpr/add | solution.py:25
  (62 shorter events, 59.0 us)
Async XLA Ops:
  7.2 7.1 %copy-start.2 = (bf16[128,2048]{1,0:T(8,128)(2,1)S(1)}, bf16[128,2048]{1,0:T(8,128)(2,1)}, u32[]{:S(2)}) copy-start(bf16[128,2048]{1,0:T(8,128)(2,1)} %param.15) | copy-start | bytes 1572868
  7.2 319.4 %all-reduce.2.cloned.1.call-start = ((), (), s32[]{:S(2)}) async-start(), calls=%async_computation | async-start | bytes 2097152 | tf_op jit(solution)/shard_map/psum | solution.py:84
  9.3 16.0 %collective-permute-start = (bf16[127,2048]{1,0:T(8,128)(2,1)S(1)}, bf16[127,2048]{1,0:T(8,128)(2,1)S(1)}, u32[]{:S(2)}, u32[]{:S(2)}) collective-permute-start(bf16[127,2048]{1,0:T(8,128)(2,1)S(1)} %slice.8), channel_id=1, source_target_pairs={{0,4},{4,8},{8,12},{12,16},{16,20},{20,24},{24,28},{1,5},{5,9},{9,... | collective-permute-start | bytes 1560584 | tf_op jit(solution)/shard_map/ppermute | solution.py:14
  25.7 87.4 %copy-start = (bf16[256,2048]{1,0:T(8,128)(2,1)S(1)}, bf16[256,2048]{1,0:T(8,128)(2,1)}, u32[]{:S(2)}) copy-start(bf16[256,2048]{1,0:T(8,128)(2,1)} %param.12) | copy-start | bytes 3145732
  113.0 7.7 %copy-start.3 = (f32[2048]{0:T(1024)S(1)}, f32[2048]{0:T(1024)}, u32[]{:S(2)}) copy-start(f32[2048]{0:T(1024)} %param.16) | copy-start | bytes 24580
  134.9 98.7 %collective-permute-start.1 = (bf16[127,2048]{1,0:T(8,128)(2,1)S(1)}, bf16[127,2048]{1,0:T(8,128)(2,1)}, u32[]{:S(2)}, u32[]{:S(2)}) collective-permute-start(bf16[127,2048]{1,0:T(8,128)(2,1)S(1)} %slice.9), channel_id=1, source_target_pairs={{4,0},{8,4},{12,8},{16,12},{20,16},{24,20},{28,24},{5,1},{9,5},{13... | collective-permute-start | bytes 1560584 | tf_op jit(solution)/shard_map/ppermute | solution.py:14
  234.7 88.1 %copy-start.1 = (bf16[256,2048]{1,0:T(8,128)(2,1)S(1)}, bf16[256,2048]{1,0:T(8,128)(2,1)}, u32[]{:S(2)}) copy-start(bf16[256,2048]{1,0:T(8,128)(2,1)} %param.14) | copy-start | bytes 3145732
Sparse Core Ops, SparseCore 0:
  207.0 82.6 all-reduce.1
where the time goes:
time: 338 us; the launch traced here: 336 us
  other arithmetic  229 us (68%)
  blocking collectives  38.3 us (11%)
  local copies, waits for them, and re-layouts  36.8 us (11%)
  between operations  14.1 us (4%)
  waiting for transfers between devices  10 us (3%)
  starting transfers between devices  6.41 us (2%)
    add x16, other arithmetic, tap_group_step(): running = running + weights[tap_index] * window  146 us
    reduce_sum x8, other arithmetic, filter_group_step(): jnp.sum(grad_conv.astype(jnp.float32) * window.astype(jnp.float32), 0)  62.3 us
    dynamic_slice x16, local copies, waits for them, and re-layouts, tap_group_step(): running = running + weights[tap_index] * window  28.5 us
    psum x1, blocking collectives, on_device(): filter_total, gain_total = lax.psum((filter_local, gain_local), 'ctx')  26.1 us
    ppermute x2, waiting for transfers between devices, passed_along(): return lax.ppermute(array, axis, pairs)  10 us
  transfers between devices with their start and end apart: 3, of which 1 were waited for; matrix products, arithmetic and copies ran while one was open for 49% of the time, Pallas kernels for 0%

commit v1 on v0

v1 whole, which is shorter than its diff:
```python
import math

import jax
import jax.numpy as jnp
import numpy as np
from jax import lax
from jax.sharding import PartitionSpec as P

EPS = 1e-06
F32 = jnp.float32
BF16 = jnp.bfloat16


def passed_along(array, axis, by):
    length = lax.axis_size(axis)
    pairs = [(i, i + by) for i in range(length) if 0 <= i + by < length]
    return lax.ppermute(array, axis, pairs)


def split(array):
    high = array.astype(BF16)
    return high, (array - high.astype(array.dtype)).astype(BF16)


def dft_matrices(block):
    length = 2 * block
    freq = np.concatenate([np.arange(0, block, 2), np.arange(1, block, 2)])
    at = np.arange(block)
    angle = 2.0 * np.pi * ((freq[:, None] * at[None, :]) % length) / length
    sign = np.where(at % 2 == 0, 1.0, -1.0)
    real, imag = np.cos(angle), -np.sin(angle)
    imag[0] = sign
    forward = np.concatenate([real, imag], 0)
    back = np.concatenate([2.0 * real, 2.0 * imag], 0)
    back[0] *= 0.5
    back[block] *= 0.5
    back = back.T / length

    def parts(matrix):
        matrix = matrix.astype(np.float32)
        high = matrix.astype(jnp.bfloat16)
        low = (matrix - high.astype(np.float32)).astype(jnp.bfloat16)
        return high, low

    fh, fl = parts(forward)
    bh, bl = parts(back)
    return np.concatenate([fh, fl], 1), np.concatenate([bh, bl, bh], 1)


def flip(spec):
    quarter = spec.shape[0] // 4
    return jnp.concatenate(
        [spec[:quarter], -spec[quarter : 2 * quarter], spec[2 * quarter : 3 * quarter], -spec[3 * quarter :]], 0
    )


def product(a, b, conj):
    half = a.shape[0] // 2
    ar, ai, br, bi = a[:half], a[half:], b[:half], b[half:]
    first = lax.broadcasted_iota(jnp.int32, ar.shape, 0) == 0
    rr, ii = ar * br, ai * bi
    if conj:
        real = jnp.where(first, rr, rr + ii)
        imag = jnp.where(first, ii, ai * br - ar * bi)
    else:
        real = jnp.where(first, rr, rr - ii)
        imag = jnp.where(first, ii, ai * br + ar * bi)
    return jnp.concatenate([real, imag], 0)


def on_device(query_proj, key_proj, value_proj, filters, norm_gain, grad_out):
    row_count, col_count = query_proj.shape
    taps = filters.shape[0]
    blocks = row_count // taps
    width = col_count * lax.axis_size("tp")
    scale = 1.0 / math.sqrt(row_count * lax.axis_size("ctx"))
    forward, back = dft_matrices(taps)

    def to_spec(rows):
        return jnp.dot(forward, jnp.concatenate([rows, rows], 0), preferred_element_type=F32)

    def from_spec(spec):
        high, low = split(spec)
        return jnp.dot(back, jnp.concatenate([high, high, low], 0), preferred_element_type=F32)

    key_wide = key_proj.astype(F32)
    value_wide = value_proj.astype(F32)
    query_wide = query_proj.astype(F32)
    key_value = (key_wide * value_wide).astype(BF16)
    before = passed_along(key_value[row_count - taps :], "ctx", 1)
    filt = to_spec(filters)
    kv_spec = [to_spec(before)] + [to_spec(key_value[b * taps : (b + 1) * taps]) for b in range(blocks)]
    kv_win = [kv_spec[b + 1] + flip(kv_spec[b]) for b in range(blocks)]
    conv_out = jnp.concatenate([from_spec(product(w, filt, False)) for w in kv_win], 0)
    gated = query_wide * conv_out
    grad_wide = grad_out.astype(F32)
    grad_scaled = grad_wide * norm_gain
    stats = lax.psum(jnp.stack([jnp.sum(gated * gated, 1), jnp.sum(grad_scaled * gated, 1)]), "tp")
    inv_rms = lax.rsqrt(stats[0] / width + EPS)
    row_mean = stats[1] * inv_rms / width
    normed = gated * inv_rms[:, None]
    mixed = (normed * norm_gain).astype(BF16)
    grad_gated = (grad_scaled - normed * row_mean[:, None]) * inv_rms[:, None]
    grad_query = (grad_gated * conv_out).astype(BF16)
    grad_conv = (grad_gated * query_wide).astype(BF16)
    after = passed_along(grad_conv[:taps], "ctx", -1)
    gc_spec = [to_spec(grad_conv[b * taps : (b + 1) * taps]) for b in range(blocks)]
    filter_spec = sum(product(gc_spec[b], kv_win[b], True) for b in range(blocks))
    filter_local = from_spec(filter_spec)
    gain_local = jnp.sum(grad_wide * normed, 0)
    total = lax.psum(jnp.concatenate([filter_local, gain_local[None]], 0), "ctx") * scale
    gc_spec = gc_spec + [to_spec(after)]
    gc_win = [gc_spec[b] + flip(gc_spec[b + 1]) for b in range(blocks)]
    grad_kv = jnp.concatenate([from_spec(product(w, filt, True)) for w in gc_win], 0)
    grad_key = (grad_kv * value_wide).astype(BF16)
    grad_value = (grad_kv * key_wide).astype(BF16)
    return (mixed, grad_query, grad_key, grad_value, total[:taps], total[taps])


def solution(mesh):
    placed = (
        P("ctx", "tp"),
        P("ctx", "tp"),
        P("ctx", "tp"),
        P(None, "tp"),
        P("tp"),
        P("ctx", "tp"),
    )
    return jax.shard_map(
        on_device,
        mesh=mesh,
        in_specs=placed,
        out_specs=(
            P("ctx", "tp"),
            P("ctx", "tp"),
            P("ctx", "tp"),
            P("ctx", "tp"),
            P(None, "tp"),
            P("tp"),
        ),
        check_vma=False,
    )
```

time: 338 us -> 160 us (0.47)
  other arithmetic: 229 us -> 17.8 us
  waiting for transfers between devices: 10 us -> 95.1 us
  blocking collectives: 38.3 us -> 5.71 us
  local copies, waits for them, and re-layouts: 36.8 us -> 6.36 us
  matrix products: 0 us -> 14.1 us
    add x16 -> x0, other arithmetic: 146 us -> none  [tap_group_step(): running = running + weights[tap_index] * window]
    psum x1, waiting for transfers between devices: 0.01 us -> 71.7 us  [on_device(): lax.psum(jnp.concatenate([filter_local, gain_local[None]], 0), 'ctx')]
    reduce_sum x10 -> x1, other arithmetic: 67 us -> 0.67 us  [on_device(): jnp.sum(gated * gated, 1)]
    psum x3 -> x1, blocking collectives: 38.3 us -> 5.71 us  [on_device(): lax.psum(jnp.stack([jnp.sum(gated * gated, 1), jnp.sum(grad_scaled * gate...]
    dynamic_slice x16 -> x0, local copies, waits for them, and re-layouts: 28.5 us -> none  [tap_group_step(): running = running + weights[tap_index] * window]
    dot_general x0 -> x29, matrix products: none -> 14.1 us  [the longest x14 8.98 us: to_spec(): jnp.dot(forward, jnp.concatenate([rows, rows], 0), preferred_element_type...]
    ppermute x2, waiting for transfers between devices: 10 us -> 23.3 us  [passed_along(): return lax.ppermute(array, axis, pairs)]
    dynamic_update_slice x8 -> x0, local copies, waits for them, and re-layouts: 5.28 us -> none  [filter_group_step(): lax.dynamic_update_slice_in_dim(total, jnp.stack(rows_out), group_index *...]
  transfers between devices with their start and end apart: 3 -> 3, of which waited for: 1 -> 3; matrix products, arithmetic and copies ran while one was open for 49% -> 6% of each run, Pallas kernels for 0% -> 0%
where the time goes in v1:
time: 160 us
  waiting for transfers between devices  95.1 us (59%)
  other arithmetic  17.8 us (11%)
  between operations  14.5 us (9%)
  matrix products  14.1 us (9%)
  starting transfers between devices  6.41 us (4%)
  local copies, waits for them, and re-layouts  6.36 us (4%)
  blocking collectives  5.71 us (4%)
    psum x1, waiting for transfers between devices, on_device(): lax.psum(jnp.concatenate([filter_local, gain_local[None]], 0), 'ctx')  71.7 us
    ppermute x2, waiting for transfers between devices, passed_along(): return lax.ppermute(array, axis, pairs)  23.3 us
    dot_general x14, matrix products, to_spec(): jnp.dot(forward, jnp.concatenate([rows, rows], 0), preferred_element_type...  8.98 us
    ppermute x2, starting transfers between devices, passed_along(): return lax.ppermute(array, axis, pairs)  6.38 us
    psum x1, blocking collectives, on_device(): lax.psum(jnp.stack([jnp.sum(gated * gated, 1), jnp.sum(grad_scaled * gate...  5.71 us
    dot_general x15, matrix products, from_spec(): jnp.dot(back, jnp.concatenate([high, high, low], 0), preferred_element_ty...  5.13 us
    unnamed x32, local copies, waits for them, and re-layouts  4.61 us
    convert_element_type x1, other arithmetic, on_device(): grad_conv = (grad_gated * query_wide).astype(BF16)  4.54 us
  transfers between devices with their start and end apart: 3, of which 3 were waited for; matrix products, arithmetic and copies ran while one was open for 6% of the time, Pallas kernels for 0%

profile of v1, /device:TPU:0, one launch (start us, length us, event | category | flops | bytes accessed | tf_op | source)
XLA Modules:
  0.0 159.9 jit_solution(13736018145283497802)
XLA Ops:
  7.2 2.0 %fusion.18 = bf16[256,2048]{1,0:T(8,128)(2,1)S(1)} fusion(bf16[256,2048]{1,0:T(8,128)(2,1)} %param.10, bf16[256,2048]{1,0:T(8,128)(2,1)} %param.9), kind=kLoop, calls=%fused_computation.42 | loop fusion | flops 2097152 | bytes 3145728 | tf_op jit(solution)/shard_map/convert_element_type | solution.py:89
  9.3 4.9 %collective-permute-start = (bf16[128,2048]{1,0:T(8,128)(2,1)S(1)}, bf16[128,2048]{1,0:T(8,128)(2,1)S(1)}, u32[]{:S(2)}, u32[]{:S(2)}) collective-permute-start(bf16[128,2048]{1,0:T(8,128)(2,1)S(1)} %slice.194), channel_id=1, source_target_pairs={{0,4},{4,8},{8,12},{12,16},{16,20},{20,24},{24,28},{1,5},{5,9},{9,... | collective-permute-start | bytes 1572872 | tf_op jit(solution)/shard_map/ppermute | solution.py:17
  14.2 0.4 fusion.67
  14.6 0.4 fusion.29
  16.0 9.4 %collective-permute-done = bf16[128,2048]{1,0:T(8,128)(2,1)S(1)} collective-permute-done((bf16[128,2048]{1,0:T(8,128)(2,1)S(1)}, bf16[128,2048]{1,0:T(8,128)(2,1)S(1)}, u32[]{:S(2)}, u32[]{:S(2)}) %collective-permute-start) | collective-permute-done | bytes 524320 | tf_op jit(solution)/shard_map/ppermute | solution.py:17
  26.3 0.7 maximum_add_fusion
  27.2 0.5 fusion.4
  27.7 1.0 subtract_select_fusion.1
  28.6 0.4 copy-done.2
  29.4 0.5 copy-done.14
  31.6 1.0 copy-done.6
  32.6 0.6 copy-done.11
  33.1 0.7 multiply_reduce_fusion
  33.8 5.7 %psum.14 = f32[2,256]{1,0:T(2,128)S(1)} all-reduce(f32[2,256]{1,0:T(2,128)S(1)} %pad_maximum_fusion.7), channel_id=1, replica_groups=mesh['ctx'=8,'tp'=4] {'tp'}, use_global_device_ids=true, to_apply=%region_2.3 | all-reduce | flops 512 | bytes 4096 | tf_op jit(solution)/shard_map/psum | solution.py:98
  39.6 4.5 %fusion.16 = (bf16[256,2048]{1,0:T(8,128)(2,1)S(1)}, bf16[256,2048]{1,0:T(8,128)(2,1)}, f32[2048]{0:T(1024)S(1)}, bf16[256,2048]{1,0:T(8,128)(2,1)}) fusion(bf16[256,2048]{1,0:T(8,128)(2,1)} %param.8, f32[256]{0:T(256)S(1)} %multiply_multiply_fusion, f32[256]{0:T(256)S(1)} %bitcast.69, f32[2048]{0:T(1024)S(1)} %copy-done.15, bf16[256,2048]{1,0:T(8,128)(2,1)} %param.13, ...), kind=kLoop, calls=%fused_computation.40 | loop fusion | flops 8910848 | bytes 7358464 | tf_op jit(solution)/shard_map/convert_element_type | solution.py:105
  44.1 1.5 collective-permute-start.1
  45.6 0.4 fusion.64
  46.1 0.4 fusion.26
  46.5 14.0 %collective-permute-done.1 = bf16[128,2048]{1,0:T(8,128)(2,1)S(1)} collective-permute-done((bf16[128,2048]{1,0:T(8,128)(2,1)S(1)}, bf16[128,2048]{1,0:T(8,128)(2,1)S(1)}, u32[]{:S(2)}, u32[]{:S(2)}) %collective-permute-start.1) | collective-permute-done | bytes 524320 | tf_op jit(solution)/shard_map/ppermute | solution.py:17
  61.5 1.8 %maximum_add_fusion.2 = (f32[256,2048]{1,0:T(8,128)}, f32[256,2048]{1,0:T(8,128)S(1)}) fusion(f32[64,2048]{1,0:T(8,128)S(1)} %get-tuple-element.35, f32[64,2048]{1,0:T(8,128)S(1)} %get-tuple-element.36, f32[64,2048]{1,0:T(8,128)S(1)} %get-tuple-element.37, f32[64,2048]{1,0:T(8,128)S(1)} %get-tuple-element.34, f32[2048,256]{0,1:T(8,128)S(1)} %fusion.26, ...), kind=kOutput, calls=%fused_computation.51 | convolution fusion | flops 136839168 | bytes 8978432 | tf_op jit(solution)/shard_map/dot_general | solution.py:80
  63.5 1.8 %maximum_add_fusion.1 = (f32[256,2048]{1,0:T(8,128)}, f32[256,2048]{1,0:T(8,128)S(1)}) fusion(f32[64,2048]{1,0:T(8,128)S(1)} %get-tuple-element.31, f32[64,2048]{1,0:T(8,128)S(1)} %get-tuple-element.32, f32[64,2048]{1,0:T(8,128)S(1)} %get-tuple-element.33, f32[64,2048]{1,0:T(8,128)S(1)} %get-tuple-element.30, f32[2048,256]{0,1:T(8,128)S(1)} %fusion.64, ...), kind=kOutput, calls=%fused_computation.49 | convolution fusion | flops 136839168 | bytes 8978432 | tf_op jit(solution)/shard_map/dot_general | solution.py:80
  65.4 1.2 add_select_fusion.1
  67.6 0.7 fusion.9
  68.3 1.2 pad_maximum_fusion.6
  69.5 0.8 copy-done.5
  70.3 3.0 %add_select_fusion.3 = (f32[128,2048]{1,0:T(8,128)S(1)}, f32[128,2048]{1,0:T(8,128)S(1)}, f32[128,2048]{1,0:T(8,128)S(1)}, f32[128,2048]{1,0:T(8,128)S(1)}) fusion(f32[256,2048]{1,0:T(8,128)} %get-tuple-element.52, f32[256,2048]{1,0:T(8,128)S(1)} %copy-done.5, pred[128]{0:T(512)(128)(4,1)S(1)} %iota_compare_fusion, f32[256,2048]{1,0:T(8,128)} %get-tuple-element.54), kind=kLoop, calls=%fused_computation.70 | loop fusion | flops 4194304 | bytes 10485888 | tf_op jit(solution)/shard_map/jit(_where)/select_n | solution.py:63
  75.2 0.9 copy-done.8
  76.4 1.9 %fusion.17 = (bf16[256,2048]{1,0:T(8,128)(2,1)}, bf16[256,2048]{1,0:T(8,128)(2,1)}) fusion(bf16[256,2048]{1,0:T(8,128)(2,1)S(1)} %copy-done.9, f32[128,2048]{1,0:T(8,128)S(1)} %fusion.10, f32[128,2048]{1,0:T(8,128)S(1)} %fusion.11, bf16[256,2048]{1,0:T(8,128)(2,1)S(1)} %copy-done.8), kind=kLoop, calls=%fused_computation.41 | loop fusion | flops 3670016 | bytes 6291456 | tf_op jit(solution)/shard_map/convert_element_type | solution.py:116
  78.3 71.7 %all-reduce.2.cloned.1.call-done = f32[129,2048]{1,0:T(8,128)} async-done(((f32[129,2048]{1,0:T(8,128)}), f32[129,2048]{1,0:T(8,128)}) %all-reduce.2.cloned.1.call-update) | async-done | bytes 1056784 | tf_op jit(solution)/shard_map/psum | solution.py:111
  150.1 1.4 broadcast_multiply_fusion
  151.4 0.6 slice.230
  152.0 1.1 slice.229
  (59 shorter events, 8.6 us)
Async XLA Ops:
  7.2 7.9 %copy-start = (bf16[128,2048]{1,0:T(8,128)(2,1)S(1)}, bf16[128,2048]{1,0:T(8,128)(2,1)}, u32[]{:S(2)}) copy-start(bf16[128,2048]{1,0:T(8,128)(2,1)} %param.11) | copy-start | bytes 1572868
  7.2 7.0 %copy-start.13 = (bf16[256,128]{1,0:T(8,128)(2,1)S(1)}, bf16[256,128]{1,0:T(8,128)(2,1)}, u32[]{:S(2)}) copy-start(bf16[256,128]{1,0:T(8,128)(2,1)} %constant.18) | copy-start | bytes 196612
  7.2 142.9 %all-reduce.2.cloned.1.call-start = ((), (), s32[]{:S(2)}) async-start(), calls=%async_computation | async-start | bytes 2228224 | tf_op jit(solution)/shard_map/psum | solution.py:111
  9.3 16.0 %collective-permute-start = (bf16[128,2048]{1,0:T(8,128)(2,1)S(1)}, bf16[128,2048]{1,0:T(8,128)(2,1)S(1)}, u32[]{:S(2)}, u32[]{:S(2)}) collective-permute-start(bf16[128,2048]{1,0:T(8,128)(2,1)S(1)} %slice.194), channel_id=1, source_target_pairs={{0,4},{4,8},{8,12},{12,16},{16,20},{20,24},{24,28},{1,5},{5,9},{9,... | collective-permute-start | bytes 1572872 | tf_op jit(solution)/shard_map/ppermute | solution.py:17
  14.6 0.9 copy-start.12
  15.9 11.7 %copy-start.4 = (f32[256,2048]{1,0:T(8,128)}, f32[256,2048]{1,0:T(8,128)S(1)}, u32[]{:S(2)}) copy-start(f32[256,2048]{1,0:T(8,128)S(1)} %convolution_add_fusion.6) | copy-start | bytes 6291460
  27.6 1.4 copy-start.2
  27.7 1.4 copy-start.7
  29.1 0.8 copy-start.14
  31.2 1.3 copy-start.10
  31.2 1.9 %copy-start.11 = (bf16[256,2048]{1,0:T(8,128)(2,1)S(1)}, bf16[256,2048]{1,0:T(8,128)(2,1)}, u32[]{:S(2)}) copy-start(bf16[256,2048]{1,0:T(8,128)(2,1)} %param.13) | copy-start | bytes 3145732
  31.2 1.9 %copy-start.15 = (f32[2048]{0:T(1024)S(1)}, f32[2048]{0:T(1024)}, u32[]{:S(2)}) copy-start(f32[2048]{0:T(1024)} %param.12) | copy-start | bytes 24580
  31.6 1.0 copy-start.6
  44.1 16.3 %collective-permute-start.1 = (bf16[128,2048]{1,0:T(8,128)(2,1)S(1)}, bf16[128,2048]{1,0:T(8,128)(2,1)S(1)}, u32[]{:S(2)}, u32[]{:S(2)}) collective-permute-start(bf16[128,2048]{1,0:T(8,128)(2,1)S(1)} %slice.211), channel_id=1, source_target_pairs={{4,0},{8,4},{12,8},{16,12},{20,16},{24,20},{28,24},{5,1},{9,5},{13... | collective-permute-start | bytes 1572872 | tf_op jit(solution)/shard_map/ppermute | solution.py:17
  63.5 1.9 %copy-start.3 = (f32[256,2048]{1,0:T(8,128)S(1)}, f32[256,2048]{1,0:T(8,128)}, u32[]{:S(2)}) copy-start(f32[256,2048]{1,0:T(8,128)} %copy-done.2) | copy-start | bytes 6291460
  68.3 2.0 %copy-start.5 = (f32[256,2048]{1,0:T(8,128)S(1)}, f32[256,2048]{1,0:T(8,128)}, u32[]{:S(2)}) copy-start(f32[256,2048]{1,0:T(8,128)} %copy-done.4) | copy-start | bytes 6291460
  74.9 1.2 copy-start.8
  74.9 1.5 copy-start.9
  76.4 76.7 %copy-start.1 = (bf16[128,2048]{1,0:T(8,128)(2,1)S(1)}, bf16[128,2048]{1,0:T(8,128)(2,1)}, u32[]{:S(2)}) copy-start(bf16[128,2048]{1,0:T(8,128)(2,1)} %param.11) | copy-start | bytes 1572868
Sparse Core Ops, SparseCore 0:
  69.6 80.3 all-reduce.1

commit v2 on v1

v2 whole, which is shorter than its diff:
```python
import functools
import math

import jax
import jax.numpy as jnp
import numpy as np
from jax import lax
from jax.experimental import pallas as pl
from jax.experimental.pallas import tpu as pltpu
from jax.sharding import PartitionSpec as P

EPS = 1e-06
F32 = jnp.float32
BF16 = jnp.bfloat16
MESH = pl.DeviceIdType.MESH
STEP = 256


def split(array):
    high = array.astype(BF16)
    return high, (array - high.astype(array.dtype)).astype(BF16)


def dft_matrices(block):
    length = 2 * block
    freq = np.concatenate([np.arange(0, block, 2), np.arange(1, block, 2)])
    at = np.arange(block)
    angle = 2.0 * np.pi * ((freq[:, None] * at[None, :]) % length) / length
    sign = np.where(at % 2 == 0, 1.0, -1.0)
    real, imag = np.cos(angle), -np.sin(angle)
    imag[0] = sign
    forward = np.concatenate([real, imag], 0)
    back = np.concatenate([2.0 * real, 2.0 * imag], 0)
    back[0] *= 0.5
    back[block] *= 0.5
    back = back.T / length

    def parts(matrix):
        matrix = matrix.astype(np.float32)
        high = matrix.astype(jnp.bfloat16)
        low = (matrix - high.astype(np.float32)).astype(jnp.bfloat16)
        return high, low

    fh, fl = parts(forward)
    bh, bl = parts(back)
    return np.concatenate([fh, fl], 1), np.concatenate([bh, bl, bh], 1)


def flip(spec):
    quarter = spec.shape[0] // 4
    return jnp.concatenate(
        [spec[:quarter], -spec[quarter : 2 * quarter], spec[2 * quarter : 3 * quarter], -spec[3 * quarter :]], 0
    )


def product(a, b, conj):
    half = a.shape[0] // 2
    ar, ai, br, bi = a[:half], a[half:], b[:half], b[half:]
    first = lax.broadcasted_iota(jnp.int32, ar.shape, 0) == 0
    rr, ii = ar * br, ai * bi
    if conj:
        real = jnp.where(first, rr, rr + ii)
        imag = jnp.where(first, ii, ai * br - ar * bi)
    else:
        real = jnp.where(first, rr, rr - ii)
        imag = jnp.where(first, ii, ai * br + ar * bi)
    return jnp.concatenate([real, imag], 0)


def kernel(n, t, inside, *refs):
    (q_ref, k_ref, v_ref, f_ref, gain_ref, go_ref, forward_ref, back_ref) = refs[:8]
    (mixed_ref, gq_ref, gk_ref, gv_ref, gf_ref, gg_ref) = refs[8:14]
    (tail, before, head, after, filt, win, gcs, conv, sq, dots, stat, stat_in, fs, rs_in, red, ag_in, gsend, g_in) = refs[14:32]
    (t_send, t_recv, h_send, h_recv, s_send, s_recv, r_send, r_recv, a_send, a_recv, g_send, g_recv) = refs[32:]
    rows, cols = q_ref.shape
    taps = f_ref.shape[0]
    blocks = rows // taps
    steps = cols // STEP
    width = cols * t
    scale = 1.0 / math.sqrt(rows * n)
    me, tp = lax.axis_index("ctx"), lax.axis_index("tp")
    has_prev, has_next = me > 0, me < n - 1

    barrier = pltpu.get_barrier_semaphore()

    def greet(axis, peer):
        pl.semaphore_signal(barrier, inc=1, device_id={axis: peer}, device_id_type=MESH)

    for d in range(1, t):
        greet("tp", lax.rem(tp + d, t))
    pl.when(has_prev)(lambda: greet("ctx", me - 1))
    pl.when(has_next)(lambda: greet("ctx", me + 1))
    if inside:
        for d in range(1, n):
            peer = lax.rem(me + d, n)
            far = jnp.logical_and(peer != me + 1, peer != me - 1)
            pl.when(far)(lambda peer=peer: greet("ctx", peer))
        pl.semaphore_wait(barrier, t - 1 + n - 1)
    else:
        pl.semaphore_wait(barrier, t - 1)
        pl.when(has_prev)(lambda: pl.semaphore_wait(barrier, 1))
        pl.when(has_next)(lambda: pl.semaphore_wait(barrier, 1))

    def remote(src, dst, send, recv, axis, peer):
        return pltpu.make_async_remote_copy(
            src_ref=src, dst_ref=dst, send_sem=send, recv_sem=recv,
            device_id={axis: peer}, device_id_type=MESH,
        )

    def tail_copy(c):
        return remote(tail.at[c], before.at[c], t_send.at[c], t_recv.at[c], "ctx", me + 1)

    def head_copy(c):
        return remote(head.at[c], after.at[c], h_send.at[c], h_recv.at[c], "ctx", me - 1)

    def to_spec(block):
        return jnp.dot(forward_ref[...], jnp.concatenate([block, block], 0), preferred_element_type=F32)

    def from_spec(spec):
        high, low = split(spec)
        return jnp.dot(back_ref[...], jnp.concatenate([high, high, low], 0), preferred_element_type=F32)

    def part(b):
        return pl.ds(b * taps, taps)

    def at(c):
        return pl.ds(pl.multiple_of(c * STEP, STEP), STEP)

    def key_value(b, c):
        return (k_ref[part(b), at(c)].astype(F32) * v_ref[part(b), at(c)].astype(F32)).astype(BF16)

    @pl.loop(0, steps)
    def _(c):
        tail[c] = key_value(blocks - 1, c)
        pl.when(has_next)(lambda: tail_copy(c).start())

    sq[...] = jnp.zeros_like(sq)
    dots[...] = jnp.zeros_like(dots)

    def forward_block(b, c):
        out = from_spec(product(win[c, b], filt[c], False))
        conv[c, part(b)] = out
        gated = q_ref[part(b), at(c)].astype(F32) * out
        graded = go_ref[part(b), at(c)].astype(F32) * gain_ref[:, at(c)] * gated
        square = gated * gated
        for i in range(STEP // 128):
            sq[part(b)] += square[:, i * 128 : (i + 1) * 128]
            dots[part(b)] += graded[:, i * 128 : (i + 1) * 128]

    @pl.loop(0, steps)
    def _(c):
        filt[c] = to_spec(f_ref[:, at(c)])
        spec = to_spec(key_value(0, c))
        win[c, 0] = spec
        for b in range(1, blocks):
            last, spec = spec, to_spec(key_value(b, c))
            win[c, b] = spec + flip(last)
            forward_block(b, c)

    @pl.when(jnp.logical_not(has_prev))
    def _():
        before[...] = jnp.zeros_like(before)

    @pl.loop(0, steps)
    def _(c):
        pl.when(has_prev)(lambda: tail_copy(c).wait_recv())
        win[c, 0] += flip(to_spec(before[c]))
        forward_block(0, c)

    lane = lax.broadcasted_iota(jnp.int32, (rows, 128), 1)
    sums = jnp.where(lane == 0, jnp.sum(sq[...], 1, keepdims=True), jnp.sum(dots[...], 1, keepdims=True))
    stat[...] = sums.T[:8]

    def stat_copy(d):
        return remote(stat, stat_in.at[d - 1], s_send.at[d - 1], s_recv.at[d - 1], "tp", lax.rem(tp + d, t))

    for d in range(1, t):
        stat_copy(d).start()
    total = stat[...]
    for d in range(1, t):
        stat_copy(d).wait_recv()
        total += stat_in[d - 1]
    total = jnp.concatenate([total] * 16, 0).T
    inv_rms = lax.rsqrt(total[:, 0:1] / width + EPS)
    row_mean = total[:, 1:2] * inv_rms / width
    sq[...] = jnp.broadcast_to(inv_rms, sq.shape)
    dots[...] = jnp.broadcast_to(row_mean, dots.shape)

    def backward_block(b, c):
        inv, mean = sq[part(b), 0:1], dots[part(b), 0:1]
        query = q_ref[part(b), at(c)].astype(F32)
        grad = go_ref[part(b), at(c)].astype(F32)
        gain = gain_ref[:, at(c)]
        out = conv[c, part(b)]
        normed = query * out * inv
        mixed_ref[part(b), at(c)] = (normed * gain).astype(BF16)
        gated = (grad * gain - normed * mean) * inv
        gq_ref[part(b), at(c)] = (gated * out).astype(BF16)
        return (gated * query).astype(BF16), jnp.sum(grad * normed, 0, keepdims=True)

    @pl.loop(0, steps)
    def _(c):
        grad_conv, gain_sum = backward_block(0, c)
        head[c] = grad_conv
        pl.when(has_prev)(lambda: head_copy(c).start())
        spec = to_spec(grad_conv)
        gcs[c, 0] = spec
        gf = product(spec, win[c, 0], True)
        for b in range(1, blocks):
            grad_conv, more = backward_block(b, c)
            gain_sum += more
            spec = to_spec(grad_conv)
            gcs[c, b] = spec
            gcs[c, b - 1] += flip(spec)
            gf += product(spec, win[c, b], True)
        gf = from_spec(gf) * scale
        gsend[:, at(c)] = gain_sum * scale
        if inside:
            size = taps // n
            rounded = gf.astype(BF16)
            for r in range(n):
                fs[r, :, at(c)] = rounded[r * size : (r + 1) * size]
        else:
            gf_ref[:, at(c)] = gf

    def rs_copy(d):
        peer = lax.rem(me + d, n)
        return remote(fs.at[peer], rs_in.at[d - 1], r_send.at[d - 1], r_recv.at[d - 1], "ctx", peer)

    def ag_copy(d):
        peer = lax.rem(me + d, n)
        return remote(red, ag_in.at[d - 1], a_send.at[d - 1], a_recv.at[d - 1], "ctx", peer)

    def gain_copy(d):
        peer = lax.rem(me + d, n)
        return remote(gsend, g_in.at[d - 1], g_send.at[d - 1], g_recv.at[d - 1], "ctx", peer)

    if inside:
        for d in range(1, n):
            rs_copy(d).start()
        for d in range(1, n):
            gain_copy(d).start()

    def last_block(b, c):
        grad_kv = from_spec(product(gcs[c, b], filt[c], True))
        gk_ref[part(b), at(c)] = (grad_kv * v_ref[part(b), at(c)].astype(F32)).astype(BF16)
        gv_ref[part(b), at(c)] = (grad_kv * k_ref[part(b), at(c)].astype(F32)).astype(BF16)

    @pl.loop(0, steps)
    def _(c):
        for b in range(blocks - 1):
            last_block(b, c)

    if inside:
        size = taps // n
        for d in range(1, n):
            rs_copy(d).wait_recv()

        @pl.loop(0, steps)
        def _(c):
            whole = fs[me, :, at(c)].astype(F32)
            for d in range(1, n):
                whole += rs_in[d - 1, :, at(c)].astype(F32)
            red[:, at(c)] = whole.astype(BF16)

        for d in range(1, n):
            ag_copy(d).start()

    @pl.when(jnp.logical_not(has_next))
    def _():
        after[...] = jnp.zeros_like(after)

    @pl.loop(0, steps)
    def _(c):
        pl.when(has_next)(lambda: head_copy(c).wait_recv())
        gcs[c, blocks - 1] += flip(to_spec(after[c]))
        last_block(blocks - 1, c)

    if inside:
        gain_sum = gsend[...]
        for d in range(1, n):
            gain_copy(d).wait_recv()
            gain_sum += g_in[d - 1]
        gg_ref[...] = gain_sum
        gf_ref[pl.ds(pl.multiple_of(me * size, size), size)] = red[...].astype(F32)
        for d in range(1, n):
            owner = lax.rem(me + n - d, n)
            ag_copy(d).wait_recv()
            gf_ref[pl.ds(pl.multiple_of(owner * size, size), size)] = ag_in[d - 1].astype(F32)
        for d in range(1, n):
            rs_copy(d).wait_send()
            gain_copy(d).wait_send()
            ag_copy(d).wait_send()
    else:
        gg_ref[...] = gsend[...]
    for d in range(1, t):
        stat_copy(d).wait_send()

    @pl.loop(0, steps)
    def _(c):
        pl.when(has_next)(lambda: tail_copy(c).wait_send())
        pl.when(has_prev)(lambda: head_copy(c).wait_send())


def on_device(query_proj, key_proj, value_proj, filters, norm_gain, grad_out):
    rows, cols = query_proj.shape
    taps = filters.shape[0]
    n, t = lax.axis_size("ctx"), lax.axis_size("tp")
    inside = taps % (16 * n) == 0
    size, peers = (taps // n, n - 1) if inside else (16, 1)
    blocks, steps = rows // taps, cols // STEP
    forward, back = dft_matrices(taps)
    wide = jax.ShapeDtypeStruct((rows, cols), BF16)
    mem = pl.BlockSpec(memory_space=pltpu.VMEM)
    dma = pltpu.SemaphoreType.DMA
    outs = pl.pallas_call(
        functools.partial(kernel, n, t, inside),
        out_shape=(wide, wide, wide, wide,
                   jax.ShapeDtypeStruct((taps, cols), F32), jax.ShapeDtypeStruct((1, cols), F32)),
        in_specs=[mem] * 8,
        out_specs=(mem,) * 6,
        scratch_shapes=[
            pltpu.VMEM((steps, taps, STEP), BF16),
            pltpu.VMEM((steps, taps, STEP), BF16),
            pltpu.VMEM((steps, taps, STEP), BF16),
            pltpu.VMEM((steps, taps, STEP), BF16),
            pltpu.VMEM((steps, 2 * taps, STEP), F32),
            pltpu.VMEM((steps, blocks, 2 * taps, STEP), F32),
            pltpu.VMEM((steps, blocks, 2 * taps, STEP), F32),
            pltpu.VMEM((steps, rows, STEP), F32),
            pltpu.VMEM((rows, 128), F32),
            pltpu.VMEM((rows, 128), F32),
            pltpu.VMEM((8, rows), F32),
            pltpu.VMEM((t - 1, 8, rows), F32),
            pltpu.VMEM((n if inside else 1, size, cols), BF16),
            pltpu.VMEM((peers, size, cols), BF16),
            pltpu.VMEM((size, cols), BF16),
            pltpu.VMEM((peers, size, cols), BF16),
            pltpu.VMEM((1, cols), F32),
            pltpu.VMEM((peers, 1, cols), F32),
        ]
        + [dma((steps,))] * 4 + [dma((t - 1,))] * 2 + [dma((peers,))] * 6,
        compiler_params=pltpu.CompilerParams(
            collective_id=0, has_side_effects=True, vmem_limit_bytes=56 * 1024 * 1024
        ),
        cost_estimate=pl.CostEstimate(flops=4_000_000_000, bytes_accessed=10_000_000, transcendentals=0),
    )(query_proj, key_proj, value_proj, filters, norm_gain[None], grad_out,
      jnp.asarray(forward), jnp.asarray(back))
    mixed, grad_query, grad_key, grad_value, grad_filter, grad_gain = outs
    if not inside:
        grad_filter, grad_gain = lax.psum((grad_filter, grad_gain), "ctx")
    return (mixed, grad_query, grad_key, grad_value, grad_filter, grad_gain[0])


def solution(mesh):
    placed = (
        P("ctx", "tp"),
        P("ctx", "tp"),
        P("ctx", "tp"),
        P(None, "tp"),
        P("tp"),
        P("ctx", "tp"),
    )
    return jax.shard_map(
        on_device,
        mesh=mesh,
        in_specs=placed,
        out_specs=(
            P("ctx", "tp"),
            P("ctx", "tp"),
            P("ctx", "tp"),
            P("ctx", "tp"),
            P(None, "tp"),
            P("tp"),
        ),
        check_vma=False,
    )
```

time: 160 us -> 77.6 us (0.48)
  the two profiles are of different devices: /device:TPU:0 before, /device:TPU:24 now
where the time goes in v2:
time: 77.6 us; the launch traced here: 77.3 us
  Pallas kernels  67.9 us (88%)
  local copies, waits for them, and re-layouts  8.78 us (11%)
    pallas_call x1, Pallas kernels, on_device(): pl.pallas_call(functools.partial(kernel, n, t, inside), out_shape=(wide,...  67.9 us
    unnamed x16, local copies, waits for them, and re-layouts  8.78 us

profile of v2, /device:TPU:24, one launch (start us, length us, event | category | flops | bytes accessed | tf_op | source)
XLA Modules:
  0.0 77.3 jit_solution(10768664601384028963)
XLA Ops:
  0.6 67.9 %shard_map.127 = (bf16[256,2048]{1,0:T(8,128)(2,1)}, bf16[256,2048]{1,0:T(8,128)(2,1)}, bf16[256,2048]{1,0:T(8,128)(2,1)}, bf16[256,2048]{1,0:T(8,128)(2,1)}, f32[128,2048]{1,0:T(8,128)}, /*index=5*/f32[1,2048]{1,0:T(1,128)}) custom-call(bf16[256,2048]{1,0:T(8,128)(2,1)} %refs_0_.1, bf16[256,2048]{1,0:T(8,128)(2,1)} %refs_1_.1, bf16[256,2048]{1,0:T(8,128)(2,1)} %refs_2_.1, ...), custom_call_target="tpu_custom_call" | custom-call | flops 4000000000 | bytes 10000000 | tf_op jit(solution)/shard_map/pallas_call | solution.py:316
  68.5 0.0 copy-start.3
  68.5 2.4 %copy.20 = bf16[256,2048]{1,0:T(8,128)(2,1)} copy(bf16[256,2048]{1,0:T(8,128)(2,1)} %get-tuple-element.24) | data formatting | bytes 2097152
  70.9 0.0 copy-done.3
  70.9 0.0 copy-start.2
  70.9 1.0 %copy.21 = bf16[256,2048]{1,0:T(8,128)(2,1)} copy(bf16[256,2048]{1,0:T(8,128)(2,1)S(1)} %copy-done.3) | data formatting | bytes 2097152
  71.9 0.6 copy-done.2
  72.5 0.0 copy-start.1
  72.5 1.0 %copy.22 = bf16[256,2048]{1,0:T(8,128)(2,1)} copy(bf16[256,2048]{1,0:T(8,128)(2,1)S(1)} %copy-done.2) | data formatting | bytes 2097152
  73.5 0.6 copy-done.1
  74.1 0.0 copy-start
  74.1 1.0 %copy.23 = bf16[256,2048]{1,0:T(8,128)(2,1)} copy(bf16[256,2048]{1,0:T(8,128)(2,1)S(1)} %copy-done.1) | data formatting | bytes 2097152
  75.1 0.6 copy-done
  75.7 0.0 copy-start.4
  75.7 1.0 %copy.24 = f32[128,2048]{1,0:T(8,128)} copy(f32[128,2048]{1,0:T(8,128)S(1)} %copy-done) | data formatting | bytes 2097152
  76.7 0.0 copy-done.4
  76.7 0.6 copy.25
Async XLA Ops:
  68.5 2.4 %copy-start.3 = (bf16[256,2048]{1,0:T(8,128)(2,1)S(1)}, bf16[256,2048]{1,0:T(8,128)(2,1)}, u32[]{:S(2)}) copy-start(bf16[256,2048]{1,0:T(8,128)(2,1)} %get-tuple-element.25) | copy-start | bytes 3145732
  70.9 1.6 %copy-start.2 = (bf16[256,2048]{1,0:T(8,128)(2,1)S(1)}, bf16[256,2048]{1,0:T(8,128)(2,1)}, u32[]{:S(2)}) copy-start(bf16[256,2048]{1,0:T(8,128)(2,1)} %get-tuple-element.26) | copy-start | bytes 3145732
  72.5 1.6 %copy-start.1 = (bf16[256,2048]{1,0:T(8,128)(2,1)S(1)}, bf16[256,2048]{1,0:T(8,128)(2,1)}, u32[]{:S(2)}) copy-start(bf16[256,2048]{1,0:T(8,128)(2,1)} %get-tuple-element.27) | copy-start | bytes 3145732
  74.1 1.6 %copy-start = (f32[128,2048]{1,0:T(8,128)S(1)}, f32[128,2048]{1,0:T(8,128)}, u32[]{:S(2)}) copy-start(f32[128,2048]{1,0:T(8,128)} %get-tuple-element.28) | copy-start | bytes 3145732
  75.7 1.0 %copy-start.4 = (f32[1,2048]{1,0:T(1,128)S(1)}, f32[1,2048]{1,0:T(1,128)}, u32[]{:S(2)}) copy-start(f32[1,2048]{1,0:T(1,128)} %get-tuple-element.17) | copy-start | bytes 24580

commit v3 on v2

--- a/solution.py
+++ b/solution.py
@@ -14,6 +14,7 @@
 BF16 = jnp.bfloat16
 MESH = pl.DeviceIdType.MESH
 STEP = 256
+PARTS = 2
 
 
 def split(array):
@@ -69,17 +70,23 @@
 
 def kernel(n, t, inside, *refs):
     (q_ref, k_ref, v_ref, f_ref, gain_ref, go_ref, forward_ref, back_ref) = refs[:8]
-    (mixed_ref, gq_ref, gk_ref, gv_ref, gf_ref, gg_ref) = refs[8:14]
+    outs = refs[8:13]
+    gg_ref = refs[13]
     (tail, before, head, after, filt, win, gcs, conv, sq, dots, stat, stat_in, fs, rs_in, red, ag_in, gsend, g_in) = refs[14:32]
-    (t_send, t_recv, h_send, h_recv, s_send, s_recv, r_send, r_recv, a_send, a_recv, g_send, g_recv) = refs[32:]
+    mixed_ref, gq_ref, gk_ref, gv_ref, gf_ref = refs[32:37]
+    (t_send, t_recv, h_send, h_recv, s_send, s_recv, r_send, r_recv, a_send, a_recv, g_send, g_recv, o_sem) = refs[37:]
     rows, cols = q_ref.shape
     taps = f_ref.shape[0]
     blocks = rows // taps
     steps = cols // STEP
+    part_steps = steps // PARTS
     width = cols * t
     scale = 1.0 / math.sqrt(rows * n)
     me, tp = lax.axis_index("ctx"), lax.axis_index("tp")
     has_prev, has_next = me > 0, me < n - 1
+
+    def leave(i):
+        return pltpu.make_async_copy((mixed_ref, gq_ref, gk_ref, gv_ref, gf_ref)[i], outs[i], o_sem.at[i])
 
     barrier = pltpu.get_barrier_semaphore()
 
@@ -198,8 +205,7 @@
         gq_ref[part(b), at(c)] = (gated * out).astype(BF16)
         return (gated * query).astype(BF16), jnp.sum(grad * normed, 0, keepdims=True)
 
-    @pl.loop(0, steps)
-    def _(c):
+    def backward_step(c):
         grad_conv, gain_sum = backward_block(0, c)
         head[c] = grad_conv
         pl.when(has_prev)(lambda: head_copy(c).start())
@@ -219,25 +225,30 @@
             size = taps // n
             rounded = gf.astype(BF16)
             for r in range(n):
-                fs[r, :, at(c)] = rounded[r * size : (r + 1) * size]
+                fs[c // part_steps, r, :, at(c % part_steps)] = rounded[r * size : (r + 1) * size]
         else:
             gf_ref[:, at(c)] = gf
 
-    def rs_copy(d):
+    def rs_copy(h, d):
         peer = lax.rem(me + d, n)
-        return remote(fs.at[peer], rs_in.at[d - 1], r_send.at[d - 1], r_recv.at[d - 1], "ctx", peer)
-
-    def ag_copy(d):
+        return remote(fs.at[h, peer], rs_in.at[h, d - 1], r_send.at[h, d - 1], r_recv.at[h, d - 1], "ctx", peer)
+
+    def ag_copy(h, d):
         peer = lax.rem(me + d, n)
-        return remote(red, ag_in.at[d - 1], a_send.at[d - 1], a_recv.at[d - 1], "ctx", peer)
+        return remote(red.at[h], ag_in.at[h, d - 1], a_send.at[h, d - 1], a_recv.at[h, d - 1], "ctx", peer)
 
     def gain_copy(d):
         peer = lax.rem(me + d, n)
         return remote(gsend, g_in.at[d - 1], g_send.at[d - 1], g_recv.at[d - 1], "ctx", peer)
 
+    for h in range(PARTS):
+        pl.loop(h * part_steps, (h + 1) * part_steps)(backward_step)
+        if inside:
+            for d in range(1, n):
+                rs_copy(h, d).start()
+    leave(0).start()
+    leave(1).start()
     if inside:
-        for d in range(1, n):
-            rs_copy(d).start()
         for d in range(1, n):
             gain_copy(d).start()
 
@@ -253,18 +264,15 @@
 
     if inside:
         size = taps // n
-        for d in range(1, n):
-            rs_copy(d).wait_recv()
-
-        @pl.loop(0, steps)
-        def _(c):
-            whole = fs[me, :, at(c)].astype(F32)
+        for h in range(PARTS):
             for d in range(1, n):
-                whole += rs_in[d - 1, :, at(c)].astype(F32)
-            red[:, at(c)] = whole.astype(BF16)
-
-        for d in range(1, n):
-            ag_copy(d).start()
+                rs_copy(h, d).wait_recv()
+            whole = fs[h, me].astype(F32)
+            for d in range(1, n):
+                whole += rs_in[h, d - 1].astype(F32)
+            red[h] = whole.astype(BF16)
+            for d in range(1, n):
+                ag_copy(h, d).start()
 
     @pl.when(jnp.logical_not(has_next))
     def _():
@@ -276,22 +284,29 @@
         gcs[c, blocks - 1] += flip(to_spec(after[c]))
         last_block(blocks - 1, c)
 
+    leave(2).start()
+    leave(3).start()
     if inside:
         gain_sum = gsend[...]
         for d in range(1, n):
             gain_copy(d).wait_recv()
             gain_sum += g_in[d - 1]
         gg_ref[...] = gain_sum
-        gf_ref[pl.ds(pl.multiple_of(me * size, size), size)] = red[...].astype(F32)
+        for h in range(PARTS):
+            span = pl.ds(h * part_steps * STEP, part_steps * STEP)
+            gf_ref[pl.ds(pl.multiple_of(me * size, size), size), span] = red[h].astype(F32)
+            for d in range(1, n):
+                owner = lax.rem(me + n - d, n)
+                ag_copy(h, d).wait_recv()
+                gf_ref[pl.ds(pl.multiple_of(owner * size, size), size), span] = ag_in[h, d - 1].astype(F32)
+        leave(4).start()
         for d in range(1, n):
-            owner = lax.rem(me + n - d, n)
-            ag_copy(d).wait_recv()
-            gf_ref[pl.ds(pl.multiple_of(owner * size, size), size)] = ag_in[d - 1].astype(F32)
-        for d in range(1, n):
-            rs_copy(d).wait_send()
             gain_copy(d).wait_send()
-            ag_copy(d).wait_send()
+            for h in range(PARTS):
+                rs_copy(h, d).wait_send()
+                ag_copy(h, d).wait_send()
     else:
+        leave(4).start()
         gg_ref[...] = gsend[...]
     for d in range(1, t):
         stat_copy(d).wait_send()
@@ -300,6 +315,17 @@
     def _(c):
         pl.when(has_next)(lambda: tail_copy(c).wait_send())
         pl.when(has_prev)(lambda: head_copy(c).wait_send())
+
+    for i in range(5):
+        leave(i).wait()
+
+
+def copies(*refs):
+    moves = [pltpu.make_async_copy(refs[i], refs[5 + i], refs[10].at[i]) for i in range(5)]
+    for move in moves:
+        move.start()
+    for move in moves:
+        move.wait()
 
 
 def on_device(query_proj, key_proj, value_proj, filters, norm_gain, grad_out):
@@ -318,7 +344,7 @@
         out_shape=(wide, wide, wide, wide,
                    jax.ShapeDtypeStruct((taps, cols), F32), jax.ShapeDtypeStruct((1, cols), F32)),
         in_specs=[mem] * 8,
-        out_specs=(mem,) * 6,
+        out_specs=(pl.BlockSpec(memory_space=pl.ANY),) * 5 + (mem,),
         scratch_shapes=[
             pltpu.VMEM((steps, taps, STEP), BF16),
             pltpu.VMEM((steps, taps, STEP), BF16),
@@ -332,21 +358,31 @@
             pltpu.VMEM((rows, 128), F32),
             pltpu.VMEM((8, rows), F32),
             pltpu.VMEM((t - 1, 8, rows), F32),
-            pltpu.VMEM((n if inside else 1, size, cols), BF16),
-            pltpu.VMEM((peers, size, cols), BF16),
-            pltpu.VMEM((size, cols), BF16),
-            pltpu.VMEM((peers, size, cols), BF16),
+            pltpu.VMEM((PARTS, n if inside else 1, size, cols // PARTS), BF16),
+            pltpu.VMEM((PARTS, peers, size, cols // PARTS), BF16),
+            pltpu.VMEM((PARTS, size, cols // PARTS), BF16),
+            pltpu.VMEM((PARTS, peers, size, cols // PARTS), BF16),
             pltpu.VMEM((1, cols), F32),
             pltpu.VMEM((peers, 1, cols), F32),
         ]
-        + [dma((steps,))] * 4 + [dma((t - 1,))] * 2 + [dma((peers,))] * 6,
+        + [pltpu.VMEM((rows, cols), BF16)] * 4 + [pltpu.VMEM((taps, cols), F32)]
+        + [dma((steps,))] * 4 + [dma((t - 1,))] * 2 + [dma((PARTS, peers))] * 4 + [dma((peers,))] * 2
+        + [dma((5,))],
         compiler_params=pltpu.CompilerParams(
             collective_id=0, has_side_effects=True, vmem_limit_bytes=56 * 1024 * 1024
         ),
         cost_estimate=pl.CostEstimate(flops=4_000_000_000, bytes_accessed=10_000_000, transcendentals=0),
     )(query_proj, key_proj, value_proj, filters, norm_gain[None], grad_out,
       jnp.asarray(forward), jnp.asarray(back))
-    mixed, grad_query, grad_key, grad_value, grad_filter, grad_gain = outs
+    hbm = pl.BlockSpec(memory_space=pl.ANY)
+    mixed, grad_query, grad_key, grad_value, grad_filter = pl.pallas_call(
+        copies,
+        out_shape=tuple(jax.ShapeDtypeStruct(a.shape, a.dtype) for a in outs[:5]),
+        in_specs=[hbm] * 5,
+        out_specs=(hbm,) * 5,
+        scratch_shapes=[dma((5,))],
+    )(*outs[:5])
+    grad_gain = outs[5]
     if not inside:
         grad_filter, grad_gain = lax.psum((grad_filter, grad_gain), "ctx")
     return (mixed, grad_query, grad_key, grad_value, grad_filter, grad_gain[0])

time: 77.6 us -> 227 us (2.93)
  the two profiles are of different devices: /device:TPU:24 before, /device:TPU:0 now
where the time goes in v3:
time: 227 us
  Pallas kernels  225 us (99%)
    pallas_call x1, Pallas kernels, on_device(): pl.pallas_call(copies, out_shape=tuple((jax.ShapeDtypeStruct(a.shape, a.d...  160 us
    pallas_call x1, Pallas kernels, on_device(): pl.pallas_call(functools.partial(kernel, n, t, inside), out_shape=(wide,...  64.9 us

profile of v3, /device:TPU:0, one launch (start us, length us, event | category | flops | bytes accessed | tf_op | source)
XLA Modules:
  0.0 226.8 jit_solution(633569319000227466)
XLA Ops:
  0.6 64.9 %shard_map.127 = (bf16[256,2048]{1,0:T(8,128)(2,1)}, bf16[256,2048]{1,0:T(8,128)(2,1)}, bf16[256,2048]{1,0:T(8,128)(2,1)}, bf16[256,2048]{1,0:T(8,128)(2,1)}, f32[128,2048]{1,0:T(8,128)}, /*index=5*/f32[1,2048]{1,0:T(1,128)}) custom-call(bf16[256,2048]{1,0:T(8,128)(2,1)} %refs_0_.1, bf16[256,2048]{1,0:T(8,128)(2,1)} %refs_1_.1, bf16[256,2048]{1,0:T(8,128)(2,1)} %refs_2_.1, ...), custom_call_target="tpu_custom_call" | custom-call | flops 4000000000 | bytes 10000000 | tf_op jit(solution)/shard_map/pallas_call | solution.py:342
  65.5 160.0 %shard_map.128 = (bf16[256,2048]{1,0:T(8,128)(2,1)}, bf16[256,2048]{1,0:T(8,128)(2,1)}, bf16[256,2048]{1,0:T(8,128)(2,1)}, bf16[256,2048]{1,0:T(8,128)(2,1)}, f32[128,2048]{1,0:T(8,128)}) custom-call(bf16[256,2048]{1,0:T(8,128)(2,1)} %get-tuple-element.17.refs_0_, bf16[256,2048]{1,0:T(8,128)(2,1)} %get-tuple-element.18.refs_1_, ...), custom_call_target="tpu_custom_call" | custom-call | tf_op jit(solution)/shard_map/pallas_call | solution.py:378
  225.5 0.0 copy-start
  225.5 0.7 copy-done
  226.2 0.6 copy.15
Async XLA Ops:
  225.5 0.7 copy-start

commit v4 on v3

--- a/solution.py
+++ b/solution.py
@@ -321,10 +321,23 @@
 
 
 def copies(*refs):
-    moves = [pltpu.make_async_copy(refs[i], refs[5 + i], refs[10].at[i]) for i in range(5)]
-    for move in moves:
+    sources, source_gain, targets, target_gain = refs[:5], refs[5], refs[6:11], refs[11]
+    held, in_sem, out_sem = refs[12:17], refs[17], refs[18]
+    inward, outward = [], []
+    for i in range(5):
+        half = sources[i].shape[0] // 2
+        for h in range(2):
+            span = pl.ds(h * half, half)
+            sems = in_sem.at[2 * i + h], out_sem.at[2 * i + h]
+            inward.append(pltpu.make_async_copy(sources[i].at[span], held[i].at[span], sems[0]))
+            outward.append(pltpu.make_async_copy(held[i].at[span], targets[i].at[span], sems[1]))
+    for move in inward:
         move.start()
-    for move in moves:
+    target_gain[...] = source_gain[...]
+    for first, second in zip(inward, outward):
+        first.wait()
+        second.start()
+    for move in outward:
         move.wait()
 
 
@@ -375,14 +388,14 @@
     )(query_proj, key_proj, value_proj, filters, norm_gain[None], grad_out,
       jnp.asarray(forward), jnp.asarray(back))
     hbm = pl.BlockSpec(memory_space=pl.ANY)
-    mixed, grad_query, grad_key, grad_value, grad_filter = pl.pallas_call(
+    mixed, grad_query, grad_key, grad_value, grad_filter, grad_gain = pl.pallas_call(
         copies,
-        out_shape=tuple(jax.ShapeDtypeStruct(a.shape, a.dtype) for a in outs[:5]),
-        in_specs=[hbm] * 5,
-        out_specs=(hbm,) * 5,
-        scratch_shapes=[dma((5,))],
-    )(*outs[:5])
-    grad_gain = outs[5]
+        out_shape=tuple(jax.ShapeDtypeStruct(a.shape, a.dtype) for a in outs),
+        in_specs=[hbm] * 5 + [mem],
+        out_specs=(hbm,) * 5 + (mem,),
+        scratch_shapes=[pltpu.VMEM(a.shape, a.dtype) for a in outs[:5]] + [dma((10,))] * 2,
+        compiler_params=pltpu.CompilerParams(vmem_limit_bytes=24 * 1024 * 1024),
+    )(*outs)
     if not inside:
         grad_filter, grad_gain = lax.psum((grad_filter, grad_gain), "ctx")
     return (mixed, grad_query, grad_key, grad_value, grad_filter, grad_gain[0])

time: 227 us -> 76.2 us (0.34)
  Pallas kernels: 225 us -> 68.3 us
  local copies, waits for them, and re-layouts: 1.29 us -> 6.81 us
    pallas_call x1, Pallas kernels: 160 us -> 3.46 us  [on_device(): pl.pallas_call(copies, out_shape=tuple((jax.ShapeDtypeStruct(a.shape, a.d...]
    unnamed x3 -> x12, local copies, waits for them, and re-layouts: 1.29 us -> 6.81 us
where the time goes in v4:
time: 76.2 us; the launch traced here: 75.8 us
  Pallas kernels  68.3 us (90%)
  local copies, waits for them, and re-layouts  6.81 us (9%)
    pallas_call x1, Pallas kernels, on_device(): pl.pallas_call(functools.partial(kernel, n, t, inside), out_shape=(wide,...  64.9 us
    unnamed x12, local copies, waits for them, and re-layouts  6.81 us
    pallas_call x1, Pallas kernels, on_device(): pl.pallas_call(copies, out_shape=tuple((jax.ShapeDtypeStruct(a.shape, a.d...  3.46 us

profile of v4, /device:TPU:0, one launch (start us, length us, event | category | flops | bytes accessed | tf_op | source)
XLA Modules:
  0.0 75.8 jit_solution(8947633419463535486)
XLA Ops:
  0.6 64.9 %shard_map.127 = (bf16[256,2048]{1,0:T(8,128)(2,1)}, bf16[256,2048]{1,0:T(8,128)(2,1)}, bf16[256,2048]{1,0:T(8,128)(2,1)}, bf16[256,2048]{1,0:T(8,128)(2,1)}, f32[128,2048]{1,0:T(8,128)}, /*index=5*/f32[1,2048]{1,0:T(1,128)}) custom-call(bf16[256,2048]{1,0:T(8,128)(2,1)} %refs_0_.1, bf16[256,2048]{1,0:T(8,128)(2,1)} %refs_1_.1, bf16[256,2048]{1,0:T(8,128)(2,1)} %refs_2_.1, ...), custom_call_target="tpu_custom_call" | custom-call | flops 4000000000 | bytes 10000000 | tf_op jit(solution)/shard_map/pallas_call | solution.py:355
  65.5 0.0 copy-start.5
  65.5 0.7 copy-done.5
  66.2 0.0 copy-start
  66.2 1.2 %copy-done = bf16[256,2048]{1,0:T(8,128)(2,1)S(1)} copy-done((bf16[256,2048]{1,0:T(8,128)(2,1)S(1)}, bf16[256,2048]{1,0:T(8,128)(2,1)}, u32[]{:S(2)}) %copy-start) | copy-done | bytes 1048600
  67.4 0.0 copy-start.1
  67.4 1.2 %copy-done.1 = bf16[256,2048]{1,0:T(8,128)(2,1)S(1)} copy-done((bf16[256,2048]{1,0:T(8,128)(2,1)S(1)}, bf16[256,2048]{1,0:T(8,128)(2,1)}, u32[]{:S(2)}) %copy-start.1) | copy-done | bytes 1048600
  68.7 0.0 copy-start.2
  68.7 1.2 %copy-done.2 = bf16[256,2048]{1,0:T(8,128)(2,1)S(1)} copy-done((bf16[256,2048]{1,0:T(8,128)(2,1)S(1)}, bf16[256,2048]{1,0:T(8,128)(2,1)}, u32[]{:S(2)}) %copy-start.2) | copy-done | bytes 1048600
  69.9 0.0 copy-start.3
  69.9 1.2 %copy-done.3 = bf16[256,2048]{1,0:T(8,128)(2,1)S(1)} copy-done((bf16[256,2048]{1,0:T(8,128)(2,1)S(1)}, bf16[256,2048]{1,0:T(8,128)(2,1)}, u32[]{:S(2)}) %copy-start.3) | copy-done | bytes 1048600
  71.1 0.0 copy-start.4
  71.1 1.2 %copy-done.4 = f32[128,2048]{1,0:T(8,128)S(1)} copy-done((f32[128,2048]{1,0:T(8,128)S(1)}, f32[128,2048]{1,0:T(8,128)}, u32[]{:S(2)}) %copy-start.4) | copy-done | bytes 1048600
  72.3 3.5 %shard_map.128 = (bf16[256,2048]{1,0:T(8,128)(2,1)}, bf16[256,2048]{1,0:T(8,128)(2,1)}, bf16[256,2048]{1,0:T(8,128)(2,1)}, bf16[256,2048]{1,0:T(8,128)(2,1)}, f32[128,2048]{1,0:T(8,128)}, /*index=5*/f32[1,2048]{1,0:T(1,128)}) custom-call(bf16[256,2048]{1,0:T(8,128)(2,1)S(1)} %copy-done, bf16[256,2048]{1,0:T(8,128)(2,1)S(1)} %copy-done.1, ...), custom_call_target="tpu_custom_call" | custom-call | tf_op jit(solution)/shard_map/pallas_call | solution.py:391
Async XLA Ops:
  65.5 0.7 copy-start.5
  66.2 1.2 %copy-start = (bf16[256,2048]{1,0:T(8,128)(2,1)S(1)}, bf16[256,2048]{1,0:T(8,128)(2,1)}, u32[]{:S(2)}) copy-start(bf16[256,2048]{1,0:T(8,128)(2,1)} %get-tuple-element.18.refs_0_) | copy-start | bytes 3145732
  67.4 1.2 %copy-start.1 = (bf16[256,2048]{1,0:T(8,128)(2,1)S(1)}, bf16[256,2048]{1,0:T(8,128)(2,1)}, u32[]{:S(2)}) copy-start(bf16[256,2048]{1,0:T(8,128)(2,1)} %get-tuple-element.19.refs_1_) | copy-start | bytes 3145732
  68.7 1.2 %copy-start.2 = (bf16[256,2048]{1,0:T(8,128)(2,1)S(1)}, bf16[256,2048]{1,0:T(8,128)(2,1)}, u32[]{:S(2)}) copy-start(bf16[256,2048]{1,0:T(8,128)(2,1)} %get-tuple-element.20.refs_2_) | copy-start | bytes 3145732
  69.9 1.2 %copy-start.3 = (bf16[256,2048]{1,0:T(8,128)(2,1)S(1)}, bf16[256,2048]{1,0:T(8,128)(2,1)}, u32[]{:S(2)}) copy-start(bf16[256,2048]{1,0:T(8,128)(2,1)} %get-tuple-element.21.refs_3_) | copy-start | bytes 3145732
  71.1 1.2 %copy-start.4 = (f32[128,2048]{1,0:T(8,128)S(1)}, f32[128,2048]{1,0:T(8,128)}, u32[]{:S(2)}) copy-start(f32[128,2048]{1,0:T(8,128)} %get-tuple-element.22.refs_4_) | copy-start | bytes 3145732

commit v5 on v4

--- a/solution.py
+++ b/solution.py
@@ -394,7 +394,7 @@
         in_specs=[hbm] * 5 + [mem],
         out_specs=(hbm,) * 5 + (mem,),
         scratch_shapes=[pltpu.VMEM(a.shape, a.dtype) for a in outs[:5]] + [dma((10,))] * 2,
-        compiler_params=pltpu.CompilerParams(vmem_limit_bytes=24 * 1024 * 1024),
+        compiler_params=pltpu.CompilerParams(vmem_limit_bytes=56 * 1024 * 1024),
     )(*outs)
     if not inside:
         grad_filter, grad_gain = lax.psum((grad_filter, grad_gain), "ctx")

time: 76.2 us -> 71.7 us (0.941)
  local copies, waits for them, and re-layouts: 6.81 us -> 0 us
  Pallas kernels: 68.3 us -> 70.9 us
    unnamed x12 -> x0, local copies, waits for them, and re-layouts: 6.81 us -> none
    pallas_call x1, Pallas kernels: 3.46 us -> 6.01 us  [on_device(): pl.pallas_call(copies, out_shape=tuple((jax.ShapeDtypeStruct(a.shape, a.d...]
where the time goes in v5:
time: 71.7 us; the launch traced here: 71.5 us
  Pallas kernels  70.9 us (99%)
    pallas_call x1, Pallas kernels, on_device(): pl.pallas_call(functools.partial(kernel, n, t, inside), out_shape=(wide,...  64.9 us
    pallas_call x1, Pallas kernels, on_device(): pl.pallas_call(copies, out_shape=tuple((jax.ShapeDtypeStruct(a.shape, a.d...  6.01 us

profile of v5, /device:TPU:0, one launch (start us, length us, event | category | flops | bytes accessed | tf_op | source)
XLA Modules:
  0.0 71.5 jit_solution(2084854431756737432)
XLA Ops:
  0.6 64.9 %shard_map.127 = (bf16[256,2048]{1,0:T(8,128)(2,1)}, bf16[256,2048]{1,0:T(8,128)(2,1)}, bf16[256,2048]{1,0:T(8,128)(2,1)}, bf16[256,2048]{1,0:T(8,128)(2,1)}, f32[128,2048]{1,0:T(8,128)}, /*index=5*/f32[1,2048]{1,0:T(1,128)}) custom-call(bf16[256,2048]{1,0:T(8,128)(2,1)} %refs_0_.1, bf16[256,2048]{1,0:T(8,128)(2,1)} %refs_1_.1, bf16[256,2048]{1,0:T(8,128)(2,1)} %refs_2_.1, ...), custom_call_target="tpu_custom_call" | custom-call | flops 4000000000 | bytes 10000000 | tf_op jit(solution)/shard_map/pallas_call | solution.py:355
  65.5 6.0 %shard_map.128 = (bf16[256,2048]{1,0:T(8,128)(2,1)}, bf16[256,2048]{1,0:T(8,128)(2,1)}, bf16[256,2048]{1,0:T(8,128)(2,1)}, bf16[256,2048]{1,0:T(8,128)(2,1)}, f32[128,2048]{1,0:T(8,128)}, /*index=5*/f32[1,2048]{1,0:T(1,128)}) custom-call(bf16[256,2048]{1,0:T(8,128)(2,1)} %get-tuple-element.18.refs_0_, bf16[256,2048]{1,0:T(8,128)(2,1)} %get-tuple-element.19.refs_1_, ...), custom_call_target="tpu_custom_call" | custom-call | tf_op jit(solution)/shard_map/pallas_call | solution.py:391
